TPU v7x, 32 devices: a whole 2x2x4 slice. The times are simulated.
32 devices in a mesh: comp: 4 (over y, x), site: 8 (over z, core).
Axes of the slice: x: 2, y: 2, z: 4, core: 2. Of those that a mesh axis runs over, the one named last changes fastest.
Arguments:
- factors: bfloat16 [24, 1024, 6144], P('comp', None, 'site'), may hold values from -0.1875 to 0.1875
- normals: bfloat16 [24, 32, 1024], P('comp', 'site'), may hold values from -6 to 6
- loadings: float32 [24, 24], replicated, may hold values from -1.25 to 1.25
- mean_ln: float32 [24, 6144], P(None, 'site'), may hold values from -4 to -0.5
- sigma: float32 [24, 6144], P(None, 'site'), may hold values from 0.3 to 1
Outputs:
- ln_motion: bfloat16 [32, 24, 6144], P(('comp', 'site'))
All inputs are finite; a program needn't handle non-finite values.
Results may differ from a plain program's by a relative error of at most 0.006.
Values may be sent and summed in bfloat16 or wider, within the bound.
A program may use at most 128 MiB of HBM per device.

v0:
```python
import functools

import jax
import jax.numpy as jnp
from jax import lax
from jax.experimental import pallas as pl
from jax.experimental.pallas import tpu as pltpu
from jax.sharding import PartitionSpec as P

MESH = pl.DeviceIdType.MESH
QUARTERS = 4
LANES = 256
PARTS = 1


def each(start, stop, step):
    if stop - start <= 8:
        for i in range(start, stop):
            step(i)
    else:
        lax.fori_loop(start, stop, lambda i, carry: (step(i), carry)[1], 0)


def kernel(
    n_comp, n_site,
    factors, normals_h, loadings_h, mean_ln, sigma, got_m,
    weights, normals, loadings, drawn, mean_v, sigma_v, mix, sent_f, got_f, sent_m,
    w_sem, in_sem, d_send, d_pass, d_recv, f_send, f_recv, m_send, m_recv, keep_sem,
):
    me_c, me_s = lax.axis_index("comp"), lax.axis_index("site")
    ks, rows, rank = normals.shape
    periods, comps = loadings.shape
    s_dev = factors.shape[2]
    chunks = s_dev // LANES
    groups = n_site // 2 // n_comp
    chips = n_site // 2
    deep = rank // QUARTERS
    f32, bf16 = jnp.float32, jnp.bfloat16

    def load_w(t, k):
        lanes = pl.ds(t * LANES, LANES)
        return pltpu.make_async_copy(
            factors.at[k, :, lanes], weights.at[t, k], w_sem.at[t, k]
        )

    mean_copy = pltpu.make_async_copy(mean_ln, mean_v, in_sem.at[0])
    sigma_copy = pltpu.make_async_copy(sigma, sigma_v, in_sem.at[1])
    normals_copy = pltpu.make_async_copy(normals_h, normals, in_sem.at[2])
    loadings_copy = pltpu.make_async_copy(loadings_h, loadings, in_sem.at[3])
    normals_copy.start()

    barrier = pltpu.get_barrier_semaphore()

    def greet_s(d):
        pl.semaphore_signal(
            barrier, inc=1, device_id={"site": me_s ^ d}, device_id_type=MESH
        )

    def greet_c(d):
        pl.semaphore_signal(
            barrier, inc=1, device_id={"comp": me_c ^ d}, device_id_type=MESH
        )

    each(1, n_site, lambda d: greet_s(n_site - d))
    each(1, n_comp, lambda d: greet_c(n_comp - d))

    loadings_copy.start()
    for t in range(chunks):
        for k in range(ks):
            load_w(t, k).start()
    mean_copy.start()
    sigma_copy.start()
    normals_copy.wait()

    for k in range(ks):
        x = normals[k].astype(f32)
        x = jnp.concatenate([x[:, q * deep:(q + 1) * deep] for q in range(QUARTERS)], axis=0)
        drawn[me_s, 16 * k:16 * (k + 1), :] = x.astype(bf16)

    pl.semaphore_wait(barrier, n_site - 1 + n_comp - 1)

    pairs = ks // 2

    def draws(slot, send_sem, peer):
        return pltpu.make_async_remote_copy(
            src_ref=drawn.at[slot], dst_ref=drawn.at[slot],
            send_sem=send_sem, recv_sem=d_recv.at[slot],
            device_id={"site": peer}, device_id_type=MESH,
        )

    def across(d):
        return draws(me_s, d_send.at[d], me_s ^ (2 * d))

    def beside(d):
        return draws(me_s ^ (2 * d), d_pass.at[d], me_s ^ 1)

    def from_beside(d):
        return draws(me_s ^ (2 * d) ^ 1, d_pass.at[d], me_s ^ 1)

    each(1, chips, lambda d: across(chips - d).start())
    beside(0).start()

    spread = (
        lax.broadcasted_iota(jnp.int32, (comps, comps * 8), 1) >> 3
        == lax.broadcasted_iota(jnp.int32, (comps, comps * 8), 0)
    ).astype(f32).astype(bf16)
    turn = lax.broadcasted_iota(jnp.int32, (periods, comps * 8), 1) & 7
    loadings_copy.wait()
    rest = loadings[...]
    for i in range(3):
        term = rest.astype(bf16)
        rest = rest - term.astype(f32)
        wide = jnp.dot(term, spread, preferred_element_type=f32)
        full = jnp.concatenate([jnp.where(turn == r, wide, 0.0) for r in range(8)], axis=0)
        mix[i * periods * 8:(i + 1) * periods * 8, :] = full.astype(bf16)

    def pass_on(d):
        beside(d).wait_recv()
        beside(d).start()

    quarter = (lax.broadcasted_iota(jnp.int32, (n_site * 16, deep), 0) >> 2) & 3
    low = lax.broadcasted_iota(jnp.int32, (chips, 8, LANES), 1) < 4

    def product(t, k):
        x = drawn[:, 16 * k:16 * (k + 1), :].reshape(n_site * 16, deep).astype(f32)
        lhs = jnp.concatenate(
            [jnp.where(quarter == q, x, 0.0).astype(bf16) for q in range(QUARTERS)], axis=1
        )
        y = jnp.dot(lhs, weights[t, k], preferred_element_type=f32)
        y = y.reshape(n_site, 2, 8, LANES)
        y = y[:, 0] + y[:, 1]
        y = y + pltpu.roll(y, 4, 1)
        y = y.reshape(chips, 2, 8, LANES)
        return jnp.where(low, y[:, 0], y[:, 1])

    def f_copy(t, d):
        peer = me_c ^ d
        at = pl.ds(pl.multiple_of(me_c * ks * 8, 16), ks * 8)
        return pltpu.make_async_remote_copy(
            src_ref=sent_f.at[t, peer], dst_ref=got_f.at[t, :, at, :],
            send_sem=f_send.at[t, d], recv_sem=f_recv.at[t, d],
            device_id={"comp": peer}, device_id_type=MESH,
        )

    def fields(j, t):
        load_w(t, 2 * j).wait()
        load_w(t, 2 * j + 1).wait()
        both = jnp.concatenate([product(t, 2 * j), product(t, 2 * j + 1)], axis=1).astype(bf16)
        sent_f[t, :, :, 16 * j:16 * (j + 1), :] = both.reshape(n_comp, groups, 16, LANES)

    def send_fields(t):
        for d in range(1, n_comp):
            f_copy(t, n_comp - d).start()
        at = pl.ds(pl.multiple_of(me_c * ks * 8, 16), ks * 8)
        got_f[t, :, at, :] = sent_f[t, me_c]

    def m_copy(t, d):
        peer = me_s ^ d
        return pltpu.make_async_remote_copy(
            src_ref=sent_m.at[t, peer], dst_ref=got_m.at[t, me_s],
            send_sem=m_send.at[t, d], recv_sem=m_recv.at[t, d],
            device_id={"site": peer}, device_id_type=MESH,
        )

    def motions(t):
        for d in range(1, n_comp):
            f_copy(t, d).wait_recv()
        mean = mean_v[:, t * LANES:(t + 1) * LANES]
        dev = sigma_v[:, t * LANES:(t + 1) * LANES]
        n = periods * 8

        def one(g):
            e = jnp.dot(mix[...], got_f[t, g], preferred_element_type=f32)
            e = (e[2 * n:] + e[n:2 * n]) + e[:n]
            m = mean[None] + dev[None] * e.reshape(8, periods, LANES)
            m = jnp.concatenate([m[:, :, :LANES // 2], m[:, :, LANES // 2:]], axis=1)
            sent_m[t, pl.ds(8 * g, 8)] = m.astype(bf16)

        each(0, groups, one)
        each(1, n_site, lambda d: m_copy(t, n_site - d).start())
        m_keep(t).start()

    def m_keep(t):
        return pltpu.make_async_copy(sent_m.at[t, me_s], got_m.at[t, me_s], keep_sem.at[t])

    each(1, chips, pass_on)
    each(0, chips, lambda d: from_beside(d).wait_recv())
    for t in range(chunks):
        for j in range(pairs):
            fields(j, t)
        send_fields(t)
    mean_copy.wait()
    sigma_copy.wait()
    for t in range(chunks):
        motions(t)

    for t in range(chunks):
        each(1, n_site, lambda d: m_copy(t, d).wait_recv())
        m_keep(t).wait()

    each(1, chips, lambda d: across(d).wait_send())
    each(0, chips, lambda d: beside(d).wait_send())
    for t in range(chunks):
        for d in range(1, n_comp):
            f_copy(t, d).wait_send()
        each(1, n_site, lambda d: m_copy(t, d).wait_send())


def arrange(blocks, out):
    chunks, slabs, rows, half = blocks.shape
    periods = rows // 2

    def one(s):
        for t in range(chunks):
            x = blocks[t, s].astype(jnp.float32)
            for h in range(2):
                at = pl.multiple_of((s * chunks + t) * 2 * half + h * half, half)
                out[0, :, pl.ds(at, half)] = x[h * periods:(h + 1) * periods].astype(out.dtype)

    each(0, slabs, one)


def body(n_comp, n_site, factors, normals, loadings, mean_ln, sigma):
    ks, rank, s_dev = factors.shape
    rows = normals.shape[1]
    periods, comps = loadings.shape
    groups = n_site // 2 // n_comp
    chunks = s_dev // LANES
    assert rows == 4 and n_comp == rows and n_site % (2 * n_comp) == 0
    assert n_site & (n_site - 1) == 0
    assert ks % 2 == 0 and periods % 8 == 0 and s_dev % LANES == 0
    bf16 = jnp.bfloat16
    dma = pltpu.SemaphoreType.DMA
    any_ = pl.BlockSpec(memory_space=pl.ANY)
    blocks = pl.pallas_call(
        functools.partial(kernel, n_comp, n_site),
        out_shape=jax.ShapeDtypeStruct((chunks, n_site, 2 * periods, LANES // 2), bf16),
        in_specs=[any_] * 5,
        out_specs=any_,
        scratch_shapes=[
            pltpu.VMEM((chunks, ks, rank, LANES), bf16),
            pltpu.VMEM(normals.shape, bf16),
            pltpu.VMEM(loadings.shape, jnp.float32),
            pltpu.VMEM((n_site, ks * 16, rank // QUARTERS), bf16),
            pltpu.VMEM((periods, s_dev), jnp.float32),
            pltpu.VMEM((periods, s_dev), jnp.float32),
            pltpu.VMEM((3 * periods * 8, comps * 8), bf16),
            pltpu.VMEM((chunks, n_comp, groups, ks * 8, LANES), bf16),
            pltpu.VMEM((chunks, groups, comps * 8, LANES), bf16),
            pltpu.VMEM((chunks, n_site, 2 * periods, LANES // 2), bf16),
            dma((chunks, ks)), dma((4,)),
            dma((n_site // 2,)), dma((n_site // 2,)), dma((n_site,)),
            dma((chunks, n_comp)), dma((chunks, n_comp)),
            dma((chunks, n_site)), dma((chunks, n_site)), dma((chunks,)),
        ],
        compiler_params=pltpu.CompilerParams(
            collective_id=0, has_side_effects=True, vmem_limit_bytes=60 * 1024 * 1024
        ),
        cost_estimate=pl.CostEstimate(
            flops=2 * ks * rows * n_site * rank * s_dev,
            bytes_accessed=2 * ks * rank * s_dev, transcendentals=0,
        ),
    )(factors, normals, loadings, mean_ln, sigma)
    part = n_site // PARTS
    return pl.pallas_call(
        arrange,
        grid=(PARTS,),
        out_shape=jax.ShapeDtypeStruct((1, periods, n_site * s_dev), bf16),
        in_specs=[pl.BlockSpec((chunks, part, 2 * periods, LANES // 2), lambda i: (0, i, 0, 0))],
        out_specs=pl.BlockSpec((1, periods, part * s_dev), lambda i: (0, 0, i)),
        compiler_params=pltpu.CompilerParams(vmem_limit_bytes=60 * 1024 * 1024),
    )(blocks)


def solution(mesh):
    in_specs = (
        P("comp", None, "site"),
        P("comp", "site", None),
        P(),
        P(None, "site"),
        P(None, "site"),
    )
    out_specs = P(("comp", "site"), None, None)
    run = functools.partial(body, mesh.shape["comp"], mesh.shape["site"])
    return jax.shard_map(run, mesh=mesh, in_specs=in_specs, out_specs=out_specs, check_vma=False)
```

profile of v0, /device:TPU:0, one launch (start us, length us, event | category | flops | bytes accessed | tf_op | source)
XLA Modules:
  0.0 27.7 jit_solution(15484409753072993408)
XLA Ops:
  0.0 25.9 %shard_map.55.blocks = bf16[3,8,48,128]{3,2,1,0:T(8,128)(2,1)} custom-call(bf16[6,1024,768]{2,1,0:T(8,128)(2,1)} %factors.1, bf16[6,4,1024]{2,1,0:T(4,128)(2,1)} %normals_h.1, f32[24,24]{1,0:T(8,128)} %loadings_h.1, f32[24,768]{1,0:T(8,128)} %mean_ln.1, f32[24,768]{1,0:T(8,128)} %sigma.1), custom_call_target="tpu_custom_call" | custom-call | flops 301989888 | bytes 9437184 | tf_op jit(solution)/shard_map/pallas_call | solution.py:235
  26.0 1.7 %shard_map.56 = bf16[1,24,6144]{2,1,0:T(8,128)(2,1)} custom-call(bf16[3,8,48,128]{3,2,1,0:T(8,128)(2,1)} %shard_map.55.blocks), custom_call_target="tpu_custom_call" | custom-call | tf_op jit(solution)/shard_map/pallas_call | solution.py:265
where the time goes:
time: 27.8 us; the launch traced here: 27.7 us
  Pallas kernels  27.7 us (100%)
    pallas_call x1, Pallas kernels, body(): pl.pallas_call(functools.partial(kernel, n_comp, n_site), out_shape=jax.S...  25.9 us
    pallas_call x1, Pallas kernels, body(): pl.pallas_call(arrange, grid=(PARTS,), out_shape=jax.ShapeDtypeStruct((1,...  1.73 us

commit v1 on v0

--- a/solution.py
+++ b/solution.py
@@ -10,7 +10,6 @@
 MESH = pl.DeviceIdType.MESH
 QUARTERS = 4
 LANES = 256
-PARTS = 1
 
 
 def each(start, stop, step):
@@ -234,7 +233,7 @@
     any_ = pl.BlockSpec(memory_space=pl.ANY)
     blocks = pl.pallas_call(
         functools.partial(kernel, n_comp, n_site),
-        out_shape=jax.ShapeDtypeStruct((chunks, n_site, 2 * periods, LANES // 2), bf16),
+        out_shape=pltpu.VMEM((chunks, n_site, 2 * periods, LANES // 2), bf16),
         in_specs=[any_] * 5,
         out_specs=any_,
         scratch_shapes=[
@@ -254,22 +253,20 @@
             dma((chunks, n_site)), dma((chunks, n_site)), dma((chunks,)),
         ],
         compiler_params=pltpu.CompilerParams(
-            collective_id=0, has_side_effects=True, vmem_limit_bytes=60 * 1024 * 1024
+            collective_id=0, has_side_effects=True, vmem_limit_bytes=40 * 1024 * 1024
         ),
         cost_estimate=pl.CostEstimate(
             flops=2 * ks * rows * n_site * rank * s_dev,
             bytes_accessed=2 * ks * rank * s_dev, transcendentals=0,
         ),
-    )(factors, normals, loadings, mean_ln, sigma)
-    part = n_site // PARTS
+    )(*(pltpu.with_memory_space_constraint(x, pltpu.HBM) for x in (factors, normals, loadings, mean_ln, sigma)))
     return pl.pallas_call(
         arrange,
-        grid=(PARTS,),
         out_shape=jax.ShapeDtypeStruct((1, periods, n_site * s_dev), bf16),
-        in_specs=[pl.BlockSpec((chunks, part, 2 * periods, LANES // 2), lambda i: (0, i, 0, 0))],
-        out_specs=pl.BlockSpec((1, periods, part * s_dev), lambda i: (0, 0, i)),
-        compiler_params=pltpu.CompilerParams(vmem_limit_bytes=60 * 1024 * 1024),
-    )(blocks)
+        in_specs=[pl.BlockSpec(memory_space=pltpu.VMEM)],
+        out_specs=pl.BlockSpec(memory_space=pltpu.VMEM),
+        compiler_params=pltpu.CompilerParams(vmem_limit_bytes=40 * 1024 * 1024),
+    )(pltpu.with_memory_space_constraint(blocks, pltpu.VMEM))
 
 
 def solution(mesh):

time: 27.8 us -> 26.8 us (0.964)
  Pallas kernels: 27.7 us -> 26.6 us
    pallas_call x2, Pallas kernels: 27.7 us -> 26.6 us  [the longest x1 25.8 us: body(): pl.pallas_call(functools.partial(kernel, n_comp, n_site), out_shape=pltpu...]
where the time goes in v1:
time: 26.8 us; the launch traced here: 26.6 us
  Pallas kernels  26.6 us (99%)
    pallas_call x1, Pallas kernels, body(): pl.pallas_call(functools.partial(kernel, n_comp, n_site), out_shape=pltpu...  25.8 us
    pallas_call x1, Pallas kernels, body(): pl.pallas_call(arrange, out_shape=jax.ShapeDtypeStruct((1, periods, n_sit...  0.77 us

profile of v1, /device:TPU:0, one launch (start us, length us, event | category | flops | bytes accessed | tf_op | source)
XLA Modules:
  0.0 26.6 jit_solution(9005875437744580727)
XLA Ops:
  0.0 25.8 %shard_map.55.blocks = bf16[3,8,48,128]{3,2,1,0:T(8,128)(2,1)S(1)} custom-call(bf16[6,1024,768]{2,1,0:T(8,128)(2,1)} %factors.1, bf16[6,4,1024]{2,1,0:T(4,128)(2,1)} %normals_h.1, f32[24,24]{1,0:T(8,128)} %loadings_h.1, f32[24,768]{1,0:T(8,128)} %mean_ln.1, f32[24,768]{1,0:T(8,128)} %sigma.1), custom_call_target="tpu_custom_call" | custom-call | flops 301989888 | bytes 9437184 | tf_op jit(solution)/shard_map/pallas_call | solution.py:234
  25.8 0.8 %shard_map.56 = bf16[1,24,6144]{2,1,0:T(8,128)(2,1)} custom-call(bf16[3,8,48,128]{3,2,1,0:T(8,128)(2,1)S(1)} %shard_map.55.blocks), custom_call_target="tpu_custom_call" | custom-call | tf_op jit(solution)/shard_map/pallas_call | solution.py:263

commit v2 on v1

--- a/solution.py
+++ b/solution.py
@@ -10,6 +10,8 @@
 MESH = pl.DeviceIdType.MESH
 QUARTERS = 4
 LANES = 256
+DRAWS = (235, 85, 190)
+MOTIONS = (239, 154, 117)
 
 
 def each(start, stop, step):
@@ -96,7 +98,15 @@
     def from_beside(d):
         return draws(me_s ^ (2 * d) ^ 1, d_pass.at[d], me_s ^ 1)
 
-    each(1, chips, lambda d: across(chips - d).start())
+    def pick(table):
+        return table // lax.shift_left(1, me_s // 2 * 2) % 4
+
+    if chips == 4:
+        first, second, last = (pick(table) for table in DRAWS)
+        across(first).start()
+        across(second).start()
+    else:
+        each(1, chips, lambda d: across(chips - d).start())
     beside(0).start()
 
     spread = (
@@ -142,8 +152,6 @@
         )
 
     def fields(j, t):
-        load_w(t, 2 * j).wait()
-        load_w(t, 2 * j + 1).wait()
         both = jnp.concatenate([product(t, 2 * j), product(t, 2 * j + 1)], axis=1).astype(bf16)
         sent_f[t, :, :, 16 * j:16 * (j + 1), :] = both.reshape(n_comp, groups, 16, LANES)
 
@@ -176,12 +184,25 @@
             sent_m[t, pl.ds(8 * g, 8)] = m.astype(bf16)
 
         each(0, groups, one)
-        each(1, n_site, lambda d: m_copy(t, n_site - d).start())
+        if chips == 4:
+            for table in MOTIONS:
+                d = pick(table) * 2
+                m_copy(t, d + 1).start()
+                m_copy(t, d).start()
+            m_copy(t, 1).start()
+        else:
+            each(1, n_site, lambda d: m_copy(t, n_site - d).start())
         m_keep(t).start()
 
     def m_keep(t):
         return pltpu.make_async_copy(sent_m.at[t, me_s], got_m.at[t, me_s], keep_sem.at[t])
 
+    if chips == 4:
+        across(first).wait_send()
+        across(last).start()
+    for t in range(chunks):
+        for k in range(ks):
+            load_w(t, k).wait()
     each(1, chips, pass_on)
     each(0, chips, lambda d: from_beside(d).wait_recv())
     for t in range(chunks):
@@ -193,16 +214,20 @@
     for t in range(chunks):
         motions(t)
 
-    for t in range(chunks):
-        each(1, n_site, lambda d: m_copy(t, d).wait_recv())
-        m_keep(t).wait()
-
-    each(1, chips, lambda d: across(d).wait_send())
+    if chips == 4:
+        across(second).wait_send()
+        across(last).wait_send()
+    else:
+        each(1, chips, lambda d: across(d).wait_send())
     each(0, chips, lambda d: beside(d).wait_send())
     for t in range(chunks):
         for d in range(1, n_comp):
             f_copy(t, d).wait_send()
+    for t in range(chunks):
+        m_keep(t).wait()
         each(1, n_site, lambda d: m_copy(t, d).wait_send())
+    for t in range(chunks):
+        each(1, n_site, lambda d: m_copy(t, d).wait_recv())
 
 
 def arrange(blocks, out):

time: 26.8 us -> 25.9 us (0.966)
  Pallas kernels: 26.6 us -> 25.7 us
    pallas_call x1, Pallas kernels: 25.8 us -> 25 us  [body(): pl.pallas_call(functools.partial(kernel, n_comp, n_site), out_shape=pltpu...]
where the time goes in v2:
time: 25.9 us; the launch traced here: 25.7 us
  Pallas kernels  25.7 us (99%)
    pallas_call x1, Pallas kernels, body(): pl.pallas_call(functools.partial(kernel, n_comp, n_site), out_shape=pltpu...  25 us
    pallas_call x1, Pallas kernels, body(): pl.pallas_call(arrange, out_shape=jax.ShapeDtypeStruct((1, periods, n_sit...  0.77 us

profile of v2, /device:TPU:0, one launch (start us, length us, event | category | flops | bytes accessed | tf_op | source)
XLA Modules:
  0.0 25.7 jit_solution(2548057252573090475)
XLA Ops:
  0.0 25.0 %shard_map.55.blocks = bf16[3,8,48,128]{3,2,1,0:T(8,128)(2,1)S(1)} custom-call(bf16[6,1024,768]{2,1,0:T(8,128)(2,1)} %factors.1, bf16[6,4,1024]{2,1,0:T(4,128)(2,1)} %normals_h.1, f32[24,24]{1,0:T(8,128)} %loadings_h.1, f32[24,768]{1,0:T(8,128)} %mean_ln.1, f32[24,768]{1,0:T(8,128)} %sigma.1), custom_call_target="tpu_custom_call" | custom-call | flops 301989888 | bytes 9437184 | tf_op jit(solution)/shard_map/pallas_call | solution.py:259
  25.0 0.8 %shard_map.56 = bf16[1,24,6144]{2,1,0:T(8,128)(2,1)} custom-call(bf16[3,8,48,128]{3,2,1,0:T(8,128)(2,1)S(1)} %shard_map.55.blocks), custom_call_target="tpu_custom_call" | custom-call | tf_op jit(solution)/shard_map/pallas_call | solution.py:288

commit v3 on v2

--- a/solution.py
+++ b/solution.py
@@ -10,8 +10,9 @@
 MESH = pl.DeviceIdType.MESH
 QUARTERS = 4
 LANES = 256
+FIELDS = (231, 186, 93)
 DRAWS = (235, 85, 190)
-MOTIONS = (239, 154, 117)
+MOTIONS = (231, 154, 125)
 
 
 def each(start, stop, step):
@@ -98,11 +99,11 @@
     def from_beside(d):
         return draws(me_s ^ (2 * d) ^ 1, d_pass.at[d], me_s ^ 1)
 
-    def pick(table):
-        return table // lax.shift_left(1, me_s // 2 * 2) % 4
+    def pick(table, at):
+        return table // lax.shift_left(1, at * 2) % 4
 
     if chips == 4:
-        first, second, last = (pick(table) for table in DRAWS)
+        first, second, last = (pick(table, me_s // 2) for table in DRAWS)
         across(first).start()
         across(second).start()
     else:
@@ -156,8 +157,8 @@
         sent_f[t, :, :, 16 * j:16 * (j + 1), :] = both.reshape(n_comp, groups, 16, LANES)
 
     def send_fields(t):
-        for d in range(1, n_comp):
-            f_copy(t, n_comp - d).start()
+        for table in FIELDS:
+            f_copy(t, pick(table, me_c)).start()
         at = pl.ds(pl.multiple_of(me_c * ks * 8, 16), ks * 8)
         got_f[t, :, at, :] = sent_f[t, me_c]
 
@@ -169,6 +170,17 @@
             device_id={"site": peer}, device_id_type=MESH,
         )
 
+    def push(t, tables):
+        for table in tables:
+            d = pick(table, me_s // 2) * 2
+            m_copy(t, d + 1).start()
+            m_copy(t, d).start()
+
+    def push_rest(t):
+        if chips == 4:
+            push(t, MOTIONS[2:])
+            m_copy(t, 1).start()
+
     def motions(t):
         for d in range(1, n_comp):
             f_copy(t, d).wait_recv()
@@ -185,11 +197,7 @@
 
         each(0, groups, one)
         if chips == 4:
-            for table in MOTIONS:
-                d = pick(table) * 2
-                m_copy(t, d + 1).start()
-                m_copy(t, d).start()
-            m_copy(t, 1).start()
+            push(t, MOTIONS[:2])
         else:
             each(1, n_site, lambda d: m_copy(t, n_site - d).start())
         m_keep(t).start()
@@ -213,6 +221,8 @@
     sigma_copy.wait()
     for t in range(chunks):
         motions(t)
+    for t in range(chunks):
+        push_rest(t)
 
     if chips == 4:
         across(second).wait_send()

time: 25.9 us -> 24.9 us (0.961)
  Pallas kernels: 25.7 us -> 24.8 us
    pallas_call x1, Pallas kernels: 25 us -> 24 us  [body(): pl.pallas_call(functools.partial(kernel, n_comp, n_site), out_shape=pltpu...]
where the time goes in v3:
time: 24.9 us; the launch traced here: 24.8 us
  Pallas kernels  24.8 us (100%)
    pallas_call x1, Pallas kernels, body(): pl.pallas_call(functools.partial(kernel, n_comp, n_site), out_shape=pltpu...  24 us
    pallas_call x1, Pallas kernels, body(): pl.pallas_call(arrange, out_shape=jax.ShapeDtypeStruct((1, periods, n_sit...  0.77 us

profile of v3, /device:TPU:0, one launch (start us, length us, event | category | flops | bytes accessed | tf_op | source)
XLA Modules:
  0.0 24.8 jit_solution(17889846757981833824)
XLA Ops:
  0.0 24.0 %shard_map.55.blocks = bf16[3,8,48,128]{3,2,1,0:T(8,128)(2,1)S(1)} custom-call(bf16[6,1024,768]{2,1,0:T(8,128)(2,1)} %factors.1, bf16[6,4,1024]{2,1,0:T(4,128)(2,1)} %normals_h.1, f32[24,24]{1,0:T(8,128)} %loadings_h.1, f32[24,768]{1,0:T(8,128)} %mean_ln.1, f32[24,768]{1,0:T(8,128)} %sigma.1), custom_call_target="tpu_custom_call" | custom-call | flops 301989888 | bytes 9437184 | tf_op jit(solution)/shard_map/pallas_call | solution.py:269
  24.0 0.8 %shard_map.56 = bf16[1,24,6144]{2,1,0:T(8,128)(2,1)} custom-call(bf16[3,8,48,128]{3,2,1,0:T(8,128)(2,1)S(1)} %shard_map.55.blocks), custom_call_target="tpu_custom_call" | custom-call | tf_op jit(solution)/shard_map/pallas_call | solution.py:298

commit v4 on v3

--- a/solution.py
+++ b/solution.py
@@ -156,9 +156,12 @@
         both = jnp.concatenate([product(t, 2 * j), product(t, 2 * j + 1)], axis=1).astype(bf16)
         sent_f[t, :, :, 16 * j:16 * (j + 1), :] = both.reshape(n_comp, groups, 16, LANES)
 
+    def push_fields(t, tables):
+        for table in tables:
+            f_copy(t, pick(table, me_c)).start()
+
     def send_fields(t):
-        for table in FIELDS:
-            f_copy(t, pick(table, me_c)).start()
+        push_fields(t, FIELDS[:1])
         at = pl.ds(pl.multiple_of(me_c * ks * 8, 16), ks * 8)
         got_f[t, :, at, :] = sent_f[t, me_c]
 
@@ -173,8 +176,8 @@
     def push(t, tables):
         for table in tables:
             d = pick(table, me_s // 2) * 2
-            m_copy(t, d + 1).start()
-            m_copy(t, d).start()
+            m_copy(t, d + me_s % 2).start()
+            m_copy(t, d + 1 - me_s % 2).start()
 
     def push_rest(t):
         if chips == 4:
@@ -217,6 +220,9 @@
         for j in range(pairs):
             fields(j, t)
         send_fields(t)
+        if t > 0:
+            push_fields(t - 1, FIELDS[1:])
+    push_fields(chunks - 1, FIELDS[1:])
     mean_copy.wait()
     sigma_copy.wait()
     for t in range(chunks):

time: 24.9 us -> 24.6 us (0.988)
  Pallas kernels: 24.8 us -> 24.5 us
    pallas_call x1, Pallas kernels: 24 us -> 23.7 us  [body(): pl.pallas_call(functools.partial(kernel, n_comp, n_site), out_shape=pltpu...]
where the time goes in v4:
time: 24.6 us; the launch traced here: 24.5 us
  Pallas kernels  24.5 us (100%)
    pallas_call x1, Pallas kernels, body(): pl.pallas_call(functools.partial(kernel, n_comp, n_site), out_shape=pltpu...  23.7 us
    pallas_call x1, Pallas kernels, body(): pl.pallas_call(arrange, out_shape=jax.ShapeDtypeStruct((1, periods, n_sit...  0.77 us

profile of v4, /device:TPU:0, one launch (start us, length us, event | category | flops | bytes accessed | tf_op | source)
XLA Modules:
  0.0 24.5 jit_solution(12637475982375071196)
XLA Ops:
  0.0 23.7 %shard_map.55.blocks = bf16[3,8,48,128]{3,2,1,0:T(8,128)(2,1)S(1)} custom-call(bf16[6,1024,768]{2,1,0:T(8,128)(2,1)} %factors.1, bf16[6,4,1024]{2,1,0:T(4,128)(2,1)} %normals_h.1, f32[24,24]{1,0:T(8,128)} %loadings_h.1, f32[24,768]{1,0:T(8,128)} %mean_ln.1, f32[24,768]{1,0:T(8,128)} %sigma.1), custom_call_target="tpu_custom_call" | custom-call | flops 301989888 | bytes 9437184 | tf_op jit(solution)/shard_map/pallas_call | solution.py:275
  23.7 0.8 %shard_map.56 = bf16[1,24,6144]{2,1,0:T(8,128)(2,1)} custom-call(bf16[3,8,48,128]{3,2,1,0:T(8,128)(2,1)S(1)} %shard_map.55.blocks), custom_call_target="tpu_custom_call" | custom-call | tf_op jit(solution)/shard_map/pallas_call | solution.py:304

commit v5 on v4

--- a/solution.py
+++ b/solution.py
@@ -11,7 +11,7 @@
 QUARTERS = 4
 LANES = 256
 FIELDS = (231, 186, 93)
-DRAWS = (235, 85, 190)
+DRAWS = (155, 117, 238)
 MOTIONS = (231, 154, 125)
 
 
@@ -209,7 +209,7 @@
         return pltpu.make_async_copy(sent_m.at[t, me_s], got_m.at[t, me_s], keep_sem.at[t])
 
     if chips == 4:
-        across(first).wait_send()
+        across(second).wait_send()
         across(last).start()
     for t in range(chunks):
         for k in range(ks):
@@ -231,7 +231,7 @@
         push_rest(t)
 
     if chips == 4:
-        across(second).wait_send()
+        across(first).wait_send()
         across(last).wait_send()
     else:
         each(1, chips, lambda d: across(d).wait_send())

time: 24.6 us -> 24.6 us (level)
  no operation moved by 1% of the time
where the time goes in v5:
time: 24.6 us; the launch traced here: 24.4 us
  Pallas kernels  24.4 us (99%)
    pallas_call x1, Pallas kernels, body(): pl.pallas_call(functools.partial(kernel, n_comp, n_site), out_shape=pltpu...  23.6 us
    pallas_call x1, Pallas kernels, body(): pl.pallas_call(arrange, out_shape=jax.ShapeDtypeStruct((1, periods, n_sit...  0.77 us

profile of v5, /device:TPU:0, one launch (start us, length us, event | category | flops | bytes accessed | tf_op | source)
XLA Modules:
  0.0 24.4 jit_solution(10752431171329652593)
XLA Ops:
  0.0 23.6 %shard_map.55.blocks = bf16[3,8,48,128]{3,2,1,0:T(8,128)(2,1)S(1)} custom-call(bf16[6,1024,768]{2,1,0:T(8,128)(2,1)} %factors.1, bf16[6,4,1024]{2,1,0:T(4,128)(2,1)} %normals_h.1, f32[24,24]{1,0:T(8,128)} %loadings_h.1, f32[24,768]{1,0:T(8,128)} %mean_ln.1, f32[24,768]{1,0:T(8,128)} %sigma.1), custom_call_target="tpu_custom_call" | custom-call | flops 301989888 | bytes 9437184 | tf_op jit(solution)/shard_map/pallas_call | solution.py:275
  23.6 0.8 %shard_map.56 = bf16[1,24,6144]{2,1,0:T(8,128)(2,1)} custom-call(bf16[3,8,48,128]{3,2,1,0:T(8,128)(2,1)S(1)} %shard_map.55.blocks), custom_call_target="tpu_custom_call" | custom-call | tf_op jit(solution)/shard_map/pallas_call | solution.py:304

commit v6 on v5

--- a/solution.py
+++ b/solution.py
@@ -66,13 +66,13 @@
     each(1, n_site, lambda d: greet_s(n_site - d))
     each(1, n_comp, lambda d: greet_c(n_comp - d))
 
+    normals_copy.wait()
     loadings_copy.start()
     for t in range(chunks):
         for k in range(ks):
             load_w(t, k).start()
     mean_copy.start()
     sigma_copy.start()
-    normals_copy.wait()
 
     for k in range(ks):
         x = normals[k].astype(f32)

time: 24.6 us -> 24.6 us (level)
  no operation moved by 1% of the time
where the time goes in v6:
time: 24.6 us; the launch traced here: 24.4 us
  Pallas kernels  24.4 us (99%)
    pallas_call x1, Pallas kernels, body(): pl.pallas_call(functools.partial(kernel, n_comp, n_site), out_shape=pltpu...  23.6 us
    pallas_call x1, Pallas kernels, body(): pl.pallas_call(arrange, out_shape=jax.ShapeDtypeStruct((1, periods, n_sit...  0.77 us

profile of v6, /device:TPU:0, one launch (start us, length us, event | category | flops | bytes accessed | tf_op | source)
XLA Modules:
  0.0 24.4 jit_solution(1896601285030178858)
XLA Ops:
  0.0 23.6 %shard_map.55.blocks = bf16[3,8,48,128]{3,2,1,0:T(8,128)(2,1)S(1)} custom-call(bf16[6,1024,768]{2,1,0:T(8,128)(2,1)} %factors.1, bf16[6,4,1024]{2,1,0:T(4,128)(2,1)} %normals_h.1, f32[24,24]{1,0:T(8,128)} %loadings_h.1, f32[24,768]{1,0:T(8,128)} %mean_ln.1, f32[24,768]{1,0:T(8,128)} %sigma.1), custom_call_target="tpu_custom_call" | custom-call | flops 301989888 | bytes 9437184 | tf_op jit(solution)/shard_map/pallas_call | solution.py:275
  23.6 0.8 %shard_map.56 = bf16[1,24,6144]{2,1,0:T(8,128)(2,1)} custom-call(bf16[3,8,48,128]{3,2,1,0:T(8,128)(2,1)S(1)} %shard_map.55.blocks), custom_call_target="tpu_custom_call" | custom-call | tf_op jit(solution)/shard_map/pallas_call | solution.py:304

commit v7 on v6

--- a/solution.py
+++ b/solution.py
@@ -12,7 +12,7 @@
 LANES = 256
 FIELDS = (231, 186, 93)
 DRAWS = (155, 117, 238)
-MOTIONS = (231, 154, 125)
+MOTIONS = (230, 155, 125)
 
 
 def each(start, stop, step):

time: 24.6 us -> 24.6 us (level)
  no operation moved by 1% of the time
where the time goes in v7:
time: 24.6 us; the launch traced here: 24.4 us
  Pallas kernels  24.4 us (99%)
    pallas_call x1, Pallas kernels, body(): pl.pallas_call(functools.partial(kernel, n_comp, n_site), out_shape=pltpu...  23.6 us
    pallas_call x1, Pallas kernels, body(): pl.pallas_call(arrange, out_shape=jax.ShapeDtypeStruct((1, periods, n_sit...  0.77 us

profile of v7, /device:TPU:0, one launch (start us, length us, event | category | flops | bytes accessed | tf_op | source)
XLA Modules:
  0.0 24.4 jit_solution(7868019193221659232)
XLA Ops:
  0.0 23.6 %shard_map.55.blocks = bf16[3,8,48,128]{3,2,1,0:T(8,128)(2,1)S(1)} custom-call(bf16[6,1024,768]{2,1,0:T(8,128)(2,1)} %factors.1, bf16[6,4,1024]{2,1,0:T(4,128)(2,1)} %normals_h.1, f32[24,24]{1,0:T(8,128)} %loadings_h.1, f32[24,768]{1,0:T(8,128)} %mean_ln.1, f32[24,768]{1,0:T(8,128)} %sigma.1), custom_call_target="tpu_custom_call" | custom-call | flops 301989888 | bytes 9437184 | tf_op jit(solution)/shard_map/pallas_call | solution.py:275
  23.6 0.8 %shard_map.56 = bf16[1,24,6144]{2,1,0:T(8,128)(2,1)} custom-call(bf16[3,8,48,128]{3,2,1,0:T(8,128)(2,1)S(1)} %shard_map.55.blocks), custom_call_target="tpu_custom_call" | custom-call | tf_op jit(solution)/shard_map/pallas_call | solution.py:304
